TPU v7x, 512 devices: a whole 4x8x8 slice. The times are simulated.
512 devices in a mesh: layer: 8 (over z), row: 8 (over x, core), col: 8 (over y).
Axes of the slice: x: 4, y: 8, z: 8, core: 2. Of those that a mesh axis runs over, the one named last changes fastest.
Arguments:
- c_states: float32 [8, 64, 64, 1024], P('layer', None, 'row', 'col'), may hold values from -6 to 6
- c_adjoints: float32 [8, 64, 64, 1024], P('layer', None, 'row', 'col'), may hold values from -6 to 6
- weights: bfloat16 [32, 64, 576], P('layer'), may hold values from -0.25 to 0.25
Outputs:
- new_states: float32 [8, 64, 64, 1024], P('layer', None, 'row', 'col')
- new_adjoints: float32 [8, 64, 64, 1024], P('layer', None, 'row', 'col')
- weight_grads: float32 [32, 64, 576], P('layer')
All inputs are finite; a program needn't handle non-finite values.
Results may differ from a plain program's by a relative error of at most 0.006.
Values may be sent and summed in bfloat16 or wider, within the bound.
A program may use at most 64 MiB of HBM per device.

v0:
```python
import jax
import jax.numpy as jnp
from jax import lax
from jax.sharding import PartitionSpec as P

step_size = 0.2


def with_halo(cells, sides, width):
    for axis, dim in sides:
        count = lax.axis_size(axis)
        ends = count - 1
        head = lax.slice_in_dim(cells, 0, width, axis=dim)
        tail = lax.slice_in_dim(cells, cells.shape[dim] - width, cells.shape[dim], axis=dim)
        cells = jnp.concatenate(
            [
                lax.ppermute(tail, axis, [(i, (i + 1) % count) for i in range(ends)]),
                cells,
                lax.ppermute(head, axis, [((i + 1) % count, i) for i in range(ends)]),
            ],
            axis=dim,
        )
    return cells


def from_behind(array, axis, by):
    devices = lax.axis_size(axis)
    pairs = [(i, i + by) for i in range(devices) if 0 <= i + by < devices]
    return lax.ppermute(array, axis, pairs)


def tile_patches(padded, tile_rows, tile_cols):
    shifted = [
        padded[:, row_off : row_off + tile_rows, col_off : col_off + tile_cols].reshape(
            padded.shape[0], tile_rows * tile_cols
        )
        for row_off in range(3)
        for col_off in range(3)
    ]
    return jnp.concatenate(shifted, 0)


def exact_dot(left_mat, right_mat):
    return jnp.dot(
        left_mat, right_mat, precision=lax.Precision.HIGHEST, preferred_element_type=jnp.float32
    )


def flipped(weight_mat):
    channels = weight_mat.shape[0]
    return jnp.transpose(weight_mat.reshape(channels, 9, channels)[:, ::-1, :], (2, 1, 0)).reshape(
        channels, 9 * channels
    )


def local(c_states, c_adjoints, weights):
    group_index = lax.axis_index("layer")
    group_count = lax.axis_size("layer")
    channels, tile_rows, tile_cols = c_states.shape[1:]
    pixels = tile_rows * tile_cols
    depth = weights.shape[0]
    initial_flat = c_states[0].reshape(channels, pixels)
    guess_flat = c_adjoints[0].reshape(channels, pixels)

    def advance(state, weight_mat):
        active = state.astype(jnp.bfloat16).reshape(channels, tile_rows, tile_cols)
        padded = with_halo(active, (("row", 1), ("col", 2)), 1)
        preact = jnp.dot(
            weight_mat,
            tile_patches(padded, tile_rows, tile_cols),
            preferred_element_type=jnp.float32,
        )
        return (state + step_size * jnp.tanh(preact), padded, preact)

    state = initial_flat
    for layer_pos in range(depth):
        state, _, _ = advance(state, weights[layer_pos])
    group_end = state
    summed = jnp.sum(weights[0].astype(jnp.float32).reshape(channels, 9, channels), axis=1)
    coarse_map = jnp.eye(channels, dtype=jnp.float32) + step_size * summed
    is_first = group_index == 0
    is_last = group_index == group_count - 1
    zero_map = jnp.zeros_like(coarse_map)
    blank = jnp.zeros((channels, pixels), jnp.float32)
    fwd_map = jnp.where(is_first, zero_map, coarse_map)
    fwd_offset = jnp.where(is_first, group_end, group_end - exact_dot(coarse_map, initial_flat))

    def state_turn(turn_number, carried):
        return from_behind(exact_dot(fwd_map, carried) + fwd_offset, "layer", 1)

    arrived = lax.fori_loop(0, group_count - 1, state_turn, blank)
    corrected = jnp.where(is_first, initial_flat, arrived)
    state = corrected
    trail = []
    for layer_pos in range(depth):
        state, padded, preact = advance(state, weights[layer_pos])
        trail.append((padded, preact))
    adjoint = guess_flat
    grad_list = [None] * depth
    for layer_pos in reversed(range(depth)):
        padded, preact = trail[layer_pos]
        slope = jnp.tanh(preact)
        source = (adjoint * step_size * (1.0 - slope * slope)).astype(jnp.bfloat16)
        source_pad = with_halo(
            source.reshape(channels, tile_rows, tile_cols), (("row", 1), ("col", 2)), 1
        )
        grad_list[layer_pos] = lax.dot_general(
            source,
            tile_patches(padded, tile_rows, tile_cols),
            (((1,), (1,)), ((), ())),
            preferred_element_type=jnp.float32,
        )
        back = jnp.dot(
            flipped(weights[layer_pos]),
            tile_patches(source_pad, tile_rows, tile_cols),
            preferred_element_type=jnp.float32,
        )
        adjoint = adjoint + back
    weight_grads = lax.psum(jnp.stack(grad_list, 0), ("row", "col"))
    transposed = coarse_map.T
    back_map = jnp.where(is_last, zero_map, transposed)
    back_offset = jnp.where(is_last, adjoint, adjoint - exact_dot(transposed, guess_flat))

    def adjoint_turn(turn_number, carried):
        return from_behind(exact_dot(back_map, carried) + back_offset, "layer", -1)

    returned = lax.fori_loop(0, group_count - 1, adjoint_turn, blank)
    new_adjoint = jnp.where(is_last, guess_flat, returned)
    out_shape = (1, channels, tile_rows, tile_cols)
    return (corrected.reshape(out_shape), new_adjoint.reshape(out_shape), weight_grads)


def solution(mesh):
    placed = (
        P("layer", None, "row", "col"),
        P("layer", None, "row", "col"),
        P("layer", None, None),
    )
    return jax.shard_map(
        local,
        mesh=mesh,
        in_specs=placed,
        out_specs=(
            P("layer", None, "row", "col"),
            P("layer", None, "row", "col"),
            P("layer", None, None),
        ),
        check_vma=False,
    )
```

profile of v0, /device:TPU:1, one launch (start us, length us, event | category | flops | bytes accessed | tf_op | source)
XLA Modules:
  0.0 560.1 jit_solution(8448254401400745606)
XLA Ops:
  12.8 5.6 collective-permute-start.3
  22.8 4.6 collective-permute-done.4
  64.7 5.2 collective-permute-start.12
  74.9 4.8 collective-permute-done.13
  105.2 64.2 %while.20 = (s32[]{:T(128)}, f32[64,1024]{1,0:T(8,128)S(1)}, f32[64,64]{1,0:T(8,128)S(1)}, f32[64,1024]{1,0:T(8,128)S(1)}, s32[]{:T(128)}) while((s32[]{:T(128)}, f32[64,1024]{1,0:T(8,128)S(1)}, f32[64,64]{1,0:T(8,128)S(1)}, f32[64,1024]{1,0:T(8,128)S(1)}, s32[]{:T(128)}) %tuple.143), condition=%wide.region_2.3_spmd, body=%wide.region_1.2_spmd.sunk | while | flops 50397184 | bytes 1851493 | solution.py:91
  109.6 5.8 %collective-permute-done = f32[64,1024]{1,0:T(8,128)S(1)} collective-permute-done((f32[64,1024]{1,0:T(8,128)S(1)}, f32[64,1024]{1,0:T(8,128)S(1)}, u32[]{:S(2)}, u32[]{:S(2)}) %collective-permute-start) | collective-permute-done | bytes 262176 | tf_op jit(solution)/shard_map/while/body/eval_jaxpr/ppermute | solution.py:29
  119.8 5.5 collective-permute-done
  129.8 4.5 collective-permute-done
  134.7 5.4 collective-permute-start
  152.0 5.1 collective-permute-start
  160.8 5.3 collective-permute-start
  169.5 6.1 %collective-permute-start.18 = (bf16[64,1,128]{2,1,0:T(2,128)(2,1)S(1)}, bf16[64,1,128]{2,1,0:T(2,128)(2,1)S(1)}, u32[]{:S(2)}, u32[]{:S(2)}) collective-permute-start(bf16[64,1,128]{2,1,0:T(2,128)(2,1)S(1)} %get-tuple-element.215), channel_id=1, source_target_pairs={{0,8},{8,16},{16,24},{24,32},{32,40},{40,48},{48,56},{1,9},{9,17},... | collective-permute-start | bytes 49160 | tf_op jit(solution)/shard_map/ppermute | solution.py:17
  211.0 4.6 collective-permute-done.25
  288.2 6.2 %collective-permute-done.37 = bf16[64,10,1]{2,1,0:T(8,128)(2,1)S(1)} collective-permute-done((bf16[64,10,1]{2,1,0:T(8,128)(2,1)}, bf16[64,10,1]{2,1,0:T(8,128)(2,1)S(1)}, u32[]{:S(2)}, u32[]{:S(2)}) %collective-permute-start.37) | collective-permute-done | bytes 1312 | tf_op jit(solution)/shard_map/ppermute | solution.py:19
  362.3 4.5 collective-permute-done.49
  369.2 71.1 %while.21 = (s32[]{:T(128)}, f32[64,1024]{1,0:T(8,128)S(1)}, f32[64,64]{1,0:T(8,128)S(1)}, f32[64,1024]{1,0:T(8,128)S(1)}, s32[]{:T(128)}) while((s32[]{:T(128)}, f32[64,1024]{1,0:T(8,128)S(1)}, f32[64,64]{1,0:T(8,128)S(1)}, f32[64,1024]{1,0:T(8,128)S(1)}, s32[]{:T(128)}) %tuple.146), condition=%wide.region_4.5_spmd, body=%wide.region_3.4_spmd.sunk | while | flops 50397184 | bytes 1851493 | solution.py:127
  370.9 10.6 %collective-permute-done.1 = f32[64,1024]{1,0:T(8,128)S(1)} collective-permute-done((f32[64,1024]{1,0:T(8,128)S(1)}, f32[64,1024]{1,0:T(8,128)S(1)}, u32[]{:S(2)}, u32[]{:S(2)}) %collective-permute-start.1) | collective-permute-done | bytes 262176 | tf_op jit(solution)/shard_map/while/body/eval_jaxpr/ppermute | solution.py:29
  383.2 10.7 %collective-permute-done.1 = f32[64,1024]{1,0:T(8,128)S(1)} collective-permute-done((f32[64,1024]{1,0:T(8,128)S(1)}, f32[64,1024]{1,0:T(8,128)S(1)}, u32[]{:S(2)}, u32[]{:S(2)}) %collective-permute-start.1) | collective-permute-done | bytes 262176 | tf_op jit(solution)/shard_map/while/body/eval_jaxpr/ppermute | solution.py:29
  395.6 10.1 %collective-permute-done.1 = f32[64,1024]{1,0:T(8,128)S(1)} collective-permute-done((f32[64,1024]{1,0:T(8,128)S(1)}, f32[64,1024]{1,0:T(8,128)S(1)}, u32[]{:S(2)}, u32[]{:S(2)}) %collective-permute-start.1) | collective-permute-done | bytes 262176 | tf_op jit(solution)/shard_map/while/body/eval_jaxpr/ppermute | solution.py:29
  407.3 9.0 %collective-permute-done.1 = f32[64,1024]{1,0:T(8,128)S(1)} collective-permute-done((f32[64,1024]{1,0:T(8,128)S(1)}, f32[64,1024]{1,0:T(8,128)S(1)}, u32[]{:S(2)}, u32[]{:S(2)}) %collective-permute-start.1) | collective-permute-done | bytes 262176 | tf_op jit(solution)/shard_map/while/body/eval_jaxpr/ppermute | solution.py:29
  418.0 6.4 %collective-permute-done.1 = f32[64,1024]{1,0:T(8,128)S(1)} collective-permute-done((f32[64,1024]{1,0:T(8,128)S(1)}, f32[64,1024]{1,0:T(8,128)S(1)}, u32[]{:S(2)}, u32[]{:S(2)}) %collective-permute-start.1) | collective-permute-done | bytes 262176 | tf_op jit(solution)/shard_map/while/body/eval_jaxpr/ppermute | solution.py:29
  426.1 5.8 %collective-permute-done.1 = f32[64,1024]{1,0:T(8,128)S(1)} collective-permute-done((f32[64,1024]{1,0:T(8,128)S(1)}, f32[64,1024]{1,0:T(8,128)S(1)}, u32[]{:S(2)}, u32[]{:S(2)}) %collective-permute-start.1) | collective-permute-done | bytes 262176 | tf_op jit(solution)/shard_map/while/body/eval_jaxpr/ppermute | solution.py:29
  433.5 6.8 %collective-permute-done.1 = f32[64,1024]{1,0:T(8,128)S(1)} collective-permute-done((f32[64,1024]{1,0:T(8,128)S(1)}, f32[64,1024]{1,0:T(8,128)S(1)}, u32[]{:S(2)}, u32[]{:S(2)}) %collective-permute-start.1) | collective-permute-done | bytes 262176 | tf_op jit(solution)/shard_map/while/body/eval_jaxpr/ppermute | solution.py:29
  441.1 110.2 %all-reduce.2.cloned.1.call-done = f32[4,64,576]{2,1,0:T(8,128)} async-done(((f32[4,64,576]{2,1,0:T(8,128)}), f32[4,64,576]{2,1,0:T(8,128)}) %all-reduce.2.cloned.1.call-update) | async-done | bytes 589840 | tf_op jit(solution)/shard_map/psum | solution.py:119
  (400 shorter events, 300.9 us)
Async XLA Ops:
  7.2 544.2 %all-reduce.2.cloned.1.call-start = ((), (), s32[]{:S(2)}) async-start(), calls=%async_computation | async-start | bytes 1310720 | tf_op jit(solution)/shard_map/psum | solution.py:119
  8.2 10.1 %collective-permute-start.2 = (bf16[64,1,128]{2,1,0:T(2,128)(2,1)S(1)}, bf16[64,1,128]{2,1,0:T(2,128)(2,1)S(1)}, u32[]{:S(2)}, u32[]{:S(2)}) collective-permute-start(bf16[64,1,128]{2,1,0:T(2,128)(2,1)S(1)} %get-tuple-element.223), channel_id=1, source_target_pairs={{0,8},{8,16},{16,24},{24,32},{32,40},{40,48},{48,56},{1,9},{9,17},... | collective-permute-start | bytes 49160 | tf_op jit(solution)/shard_map/ppermute | solution.py:17
  21.5 10.1 %collective-permute-start.5 = (bf16[64,10,1]{2,1,0:T(8,128)(2,1)S(1)}, bf16[64,10,1]{2,1,0:T(8,128)(2,1)S(1)}, u32[]{:S(2)}, u32[]{:S(2)}) collective-permute-start(bf16[64,10,1]{2,1,0:T(8,128)(2,1)S(1)} %get-tuple-element.175), channel_id=1, source_target_pairs={{1,0},{2,1},{3,2},{4,3},{5,4},{6,5},{7,6},{9,8},{10,9},{11,10},{12... | collective-permute-start | bytes 3848 | tf_op jit(solution)/shard_map/ppermute | solution.py:19
  64.7 9.7 %collective-permute-start.12 = (bf16[64,10,1]{2,1,0:T(8,128)(2,1)S(1)}, bf16[64,10,1]{2,1,0:T(8,128)(2,1)S(1)}, u32[]{:S(2)}, u32[]{:S(2)}) collective-permute-start(bf16[64,10,1]{2,1,0:T(8,128)(2,1)S(1)} %get-tuple-element.172), channel_id=1, source_target_pairs={{0,1},{1,2},{2,3},{3,4},{4,5},{5,6},{6,7},{8,9},{9,10},{10,11},{11... | collective-permute-start | bytes 3848 | tf_op jit(solution)/shard_map/ppermute | solution.py:17
  70.8 8.9 %collective-permute-start.13 = (bf16[64,10,1]{2,1,0:T(8,128)(2,1)S(1)}, bf16[64,10,1]{2,1,0:T(8,128)(2,1)S(1)}, u32[]{:S(2)}, u32[]{:S(2)}) collective-permute-start(bf16[64,10,1]{2,1,0:T(8,128)(2,1)S(1)} %get-tuple-element.171), channel_id=1, source_target_pairs={{1,0},{2,1},{3,2},{4,3},{5,4},{6,5},{7,6},{9,8},{10,9},{11,10},{12... | collective-permute-start | bytes 3848 | tf_op jit(solution)/shard_map/ppermute | solution.py:19
  105.6 9.8 %collective-permute-start = (f32[64,1024]{1,0:T(8,128)S(1)}, f32[64,1024]{1,0:T(8,128)S(1)}, u32[]{:S(2)}, u32[]{:S(2)}) collective-permute-start(f32[64,1024]{1,0:T(8,128)S(1)} %convolution_add_fusion.4), channel_id=1, source_target_pairs={{0,64},{64,128},{128,192},{192,256},{256,320},{320,384},{384,448},... | collective-permute-start | bytes 786440 | tf_op jit(solution)/shard_map/while/body/eval_jaxpr/ppermute | solution.py:29
  115.8 9.5 %collective-permute-start = (f32[64,1024]{1,0:T(8,128)S(1)}, f32[64,1024]{1,0:T(8,128)S(1)}, u32[]{:S(2)}, u32[]{:S(2)}) collective-permute-start(f32[64,1024]{1,0:T(8,128)S(1)} %convolution_add_fusion.4), channel_id=1, source_target_pairs={{0,64},{64,128},{128,192},{192,256},{256,320},{320,384},{384,448},... | collective-permute-start | bytes 786440 | tf_op jit(solution)/shard_map/while/body/eval_jaxpr/ppermute | solution.py:29
  125.7 8.7 %collective-permute-start = (f32[64,1024]{1,0:T(8,128)S(1)}, f32[64,1024]{1,0:T(8,128)S(1)}, u32[]{:S(2)}, u32[]{:S(2)}) collective-permute-start(f32[64,1024]{1,0:T(8,128)S(1)} %convolution_add_fusion.4), channel_id=1, source_target_pairs={{0,64},{64,128},{128,192},{192,256},{256,320},{320,384},{384,448},... | collective-permute-start | bytes 786440 | tf_op jit(solution)/shard_map/while/body/eval_jaxpr/ppermute | solution.py:29
  134.7 9.2 %collective-permute-start = (f32[64,1024]{1,0:T(8,128)S(1)}, f32[64,1024]{1,0:T(8,128)S(1)}, u32[]{:S(2)}, u32[]{:S(2)}) collective-permute-start(f32[64,1024]{1,0:T(8,128)S(1)} %convolution_add_fusion.4), channel_id=1, source_target_pairs={{0,64},{64,128},{128,192},{192,256},{256,320},{320,384},{384,448},... | collective-permute-start | bytes 786440 | tf_op jit(solution)/shard_map/while/body/eval_jaxpr/ppermute | solution.py:29
  169.5 9.0 %collective-permute-start.18 = (bf16[64,1,128]{2,1,0:T(2,128)(2,1)S(1)}, bf16[64,1,128]{2,1,0:T(2,128)(2,1)S(1)}, u32[]{:S(2)}, u32[]{:S(2)}) collective-permute-start(bf16[64,1,128]{2,1,0:T(2,128)(2,1)S(1)} %get-tuple-element.215), channel_id=1, source_target_pairs={{0,8},{8,16},{16,24},{24,32},{32,40},{40,48},{48,56},{1,9},{9,17},... | collective-permute-start | bytes 49160 | tf_op jit(solution)/shard_map/ppermute | solution.py:17
  183.5 9.3 %collective-permute-start.21 = (bf16[64,10,1]{2,1,0:T(8,128)(2,1)S(1)}, bf16[64,10,1]{2,1,0:T(8,128)(2,1)S(1)}, u32[]{:S(2)}, u32[]{:S(2)}) collective-permute-start(bf16[64,10,1]{2,1,0:T(8,128)(2,1)S(1)} %get-tuple-element.167), channel_id=1, source_target_pairs={{1,0},{2,1},{3,2},{4,3},{5,4},{6,5},{7,6},{9,8},{10,9},{11,10},{12... | collective-permute-start | bytes 3848 | tf_op jit(solution)/shard_map/ppermute | solution.py:19
  206.1 9.6 %collective-permute-start.25 = (bf16[64,10,1]{2,1,0:T(8,128)(2,1)S(1)}, bf16[64,10,1]{2,1,0:T(8,128)(2,1)S(1)}, u32[]{:S(2)}, u32[]{:S(2)}) collective-permute-start(bf16[64,10,1]{2,1,0:T(8,128)(2,1)S(1)} %get-tuple-element.165), channel_id=1, source_target_pairs={{1,0},{2,1},{3,2},{4,3},{5,4},{6,5},{7,6},{9,8},{10,9},{11,10},{12... | collective-permute-start | bytes 3848 | tf_op jit(solution)/shard_map/ppermute | solution.py:19
  231.7 8.7 %collective-permute-start.29 = (bf16[64,10,1]{2,1,0:T(8,128)(2,1)}, bf16[64,10,1]{2,1,0:T(8,128)(2,1)S(1)}, u32[]{:S(2)}, u32[]{:S(2)}) collective-permute-start(bf16[64,10,1]{2,1,0:T(8,128)(2,1)} %get-tuple-element.163), channel_id=1, source_target_pairs={{1,0},{2,1},{3,2},{4,3},{5,4},{6,5},{7,6},{9,8},{10,9},{11,10},{12... | collective-permute-start | bytes 3848 | tf_op jit(solution)/shard_map/ppermute | solution.py:19
  255.7 8.7 %collective-permute-start.33 = (bf16[64,10,1]{2,1,0:T(8,128)(2,1)}, bf16[64,10,1]{2,1,0:T(8,128)(2,1)S(1)}, u32[]{:S(2)}, u32[]{:S(2)}) collective-permute-start(bf16[64,10,1]{2,1,0:T(8,128)(2,1)} %get-tuple-element.161), channel_id=1, source_target_pairs={{1,0},{2,1},{3,2},{4,3},{5,4},{6,5},{7,6},{9,8},{10,9},{11,10},{12... | collective-permute-start | bytes 3848 | tf_op jit(solution)/shard_map/ppermute | solution.py:19
  277.7 8.7 %collective-permute-start.36 = (bf16[64,10,1]{2,1,0:T(8,128)(2,1)}, bf16[64,10,1]{2,1,0:T(8,128)(2,1)}, u32[]{:S(2)}, u32[]{:S(2)}) collective-permute-start(bf16[64,10,1]{2,1,0:T(8,128)(2,1)} %get-tuple-element.160), channel_id=1, source_target_pairs={{0,1},{1,2},{2,3},{3,4},{4,5},{5,6},{6,7},{8,9},{9,10},{10,11},{11... | collective-permute-start | bytes 3848 | tf_op jit(solution)/shard_map/ppermute | solution.py:17
  285.2 9.3 %collective-permute-start.37 = (bf16[64,10,1]{2,1,0:T(8,128)(2,1)}, bf16[64,10,1]{2,1,0:T(8,128)(2,1)S(1)}, u32[]{:S(2)}, u32[]{:S(2)}) collective-permute-start(bf16[64,10,1]{2,1,0:T(8,128)(2,1)} %get-tuple-element.159), channel_id=1, source_target_pairs={{1,0},{2,1},{3,2},{4,3},{5,4},{6,5},{7,6},{9,8},{10,9},{11,10},{12... | collective-permute-start | bytes 3848 | tf_op jit(solution)/shard_map/ppermute | solution.py:19
  298.8 9.9 %collective-permute-start.38 = (bf16[64,1,128]{2,1,0:T(2,128)(2,1)}, bf16[64,1,128]{2,1,0:T(2,128)(2,1)S(1)}, u32[]{:S(2)}, u32[]{:S(2)}) collective-permute-start(bf16[64,1,128]{2,1,0:T(2,128)(2,1)} %get-tuple-element.205), channel_id=1, source_target_pairs={{0,8},{8,16},{16,24},{24,32},{32,40},{40,48},{48,56},{1,9},{9,17},... | collective-permute-start | bytes 49160 | tf_op jit(solution)/shard_map/ppermute | solution.py:17
  312.0 10.1 %collective-permute-start.41 = (bf16[64,10,1]{2,1,0:T(8,128)(2,1)S(1)}, bf16[64,10,1]{2,1,0:T(8,128)(2,1)S(1)}, u32[]{:S(2)}, u32[]{:S(2)}) collective-permute-start(bf16[64,10,1]{2,1,0:T(8,128)(2,1)S(1)} %get-tuple-element.157), channel_id=1, source_target_pairs={{1,0},{2,1},{3,2},{4,3},{5,4},{6,5},{7,6},{9,8},{10,9},{11,10},{12... | collective-permute-start | bytes 3848 | tf_op jit(solution)/shard_map/ppermute | solution.py:19
  335.4 9.0 %collective-permute-start.45 = (bf16[64,10,1]{2,1,0:T(8,128)(2,1)S(1)}, bf16[64,10,1]{2,1,0:T(8,128)(2,1)S(1)}, u32[]{:S(2)}, u32[]{:S(2)}) collective-permute-start(bf16[64,10,1]{2,1,0:T(8,128)(2,1)S(1)} %get-tuple-element.155), channel_id=1, source_target_pairs={{1,0},{2,1},{3,2},{4,3},{5,4},{6,5},{7,6},{9,8},{10,9},{11,10},{12... | collective-permute-start | bytes 3848 | tf_op jit(solution)/shard_map/ppermute | solution.py:19
  357.8 9.0 %collective-permute-start.49 = (bf16[64,10,1]{2,1,0:T(8,128)(2,1)S(1)}, bf16[64,10,1]{2,1,0:T(8,128)(2,1)S(1)}, u32[]{:S(2)}, u32[]{:S(2)}) collective-permute-start(bf16[64,10,1]{2,1,0:T(8,128)(2,1)S(1)} %get-tuple-element.153), channel_id=1, source_target_pairs={{1,0},{2,1},{3,2},{4,3},{5,4},{6,5},{7,6},{9,8},{10,9},{11,10},{12... | collective-permute-start | bytes 3848 | tf_op jit(solution)/shard_map/ppermute | solution.py:19
  369.6 11.9 %collective-permute-start.1 = (f32[64,1024]{1,0:T(8,128)S(1)}, f32[64,1024]{1,0:T(8,128)S(1)}, u32[]{:S(2)}, u32[]{:S(2)}) collective-permute-start(f32[64,1024]{1,0:T(8,128)S(1)} %convolution_add_fusion.5), channel_id=1, source_target_pairs={{64,0},{128,64},{192,128},{256,192},{320,256},{384,320},{448,384},... | collective-permute-start | bytes 786440 | tf_op jit(solution)/shard_map/while/body/eval_jaxpr/ppermute | solution.py:29
  381.9 12.0 %collective-permute-start.1 = (f32[64,1024]{1,0:T(8,128)S(1)}, f32[64,1024]{1,0:T(8,128)S(1)}, u32[]{:S(2)}, u32[]{:S(2)}) collective-permute-start(f32[64,1024]{1,0:T(8,128)S(1)} %convolution_add_fusion.5), channel_id=1, source_target_pairs={{64,0},{128,64},{192,128},{256,192},{320,256},{384,320},{448,384},... | collective-permute-start | bytes 786440 | tf_op jit(solution)/shard_map/while/body/eval_jaxpr/ppermute | solution.py:29
  394.3 11.4 %collective-permute-start.1 = (f32[64,1024]{1,0:T(8,128)S(1)}, f32[64,1024]{1,0:T(8,128)S(1)}, u32[]{:S(2)}, u32[]{:S(2)}) collective-permute-start(f32[64,1024]{1,0:T(8,128)S(1)} %convolution_add_fusion.5), channel_id=1, source_target_pairs={{64,0},{128,64},{192,128},{256,192},{320,256},{384,320},{448,384},... | collective-permute-start | bytes 786440 | tf_op jit(solution)/shard_map/while/body/eval_jaxpr/ppermute | solution.py:29
  406.0 10.3 %collective-permute-start.1 = (f32[64,1024]{1,0:T(8,128)S(1)}, f32[64,1024]{1,0:T(8,128)S(1)}, u32[]{:S(2)}, u32[]{:S(2)}) collective-permute-start(f32[64,1024]{1,0:T(8,128)S(1)} %convolution_add_fusion.5), channel_id=1, source_target_pairs={{64,0},{128,64},{192,128},{256,192},{320,256},{384,320},{448,384},... | collective-permute-start | bytes 786440 | tf_op jit(solution)/shard_map/while/body/eval_jaxpr/ppermute | solution.py:29
  (66 other events, 419.7 us)
Sparse Core Ops, SparseCore 0:
  357.9 193.3 all-reduce.1
where the time goes:
time: 563 us; the launch traced here: 560 us
  waiting for transfers between devices  312 us (55%)
  starting transfers between devices  164 us (29%)
  local copies, waits for them, and re-layouts  28.5 us (5%)
  other arithmetic  24.9 us (4%)
  between operations  16.1 us (3%)
  matrix products  13.7 us (2%)
    psum x1, waiting for transfers between devices, local(): weight_grads = lax.psum(jnp.stack(grad_list, 0), ('row', 'col'))  110 us
    ppermute x14, waiting for transfers between devices, from_behind(): return lax.ppermute(array, axis, pairs)  88.8 us
    ppermute x24, waiting for transfers between devices, with_halo(): lax.ppermute(head, axis, [((i + 1) % count, i) for i in range(ends)])  78.5 us
    ppermute x24, starting transfers between devices, with_halo(): lax.ppermute(tail, axis, [(i, (i + 1) % count) for i in range(ends)])  77.9 us
    ppermute x24, starting transfers between devices, with_halo(): lax.ppermute(head, axis, [((i + 1) % count, i) for i in range(ends)])  45.4 us
    ppermute x14, starting transfers between devices, from_behind(): return lax.ppermute(array, axis, pairs)  41.1 us
    ppermute x24, waiting for transfers between devices, with_halo(): lax.ppermute(tail, axis, [(i, (i + 1) % count) for i in range(ends)])  34.7 us
    concatenate x36, other arithmetic, with_halo(): jnp.concatenate([lax.ppermute(tail, axis, [(i, (i + 1) % count) for i in...  21.9 us
  transfers between devices with their start and end apart: 63, of which 49 were waited for; matrix products, arithmetic and copies ran while one was open for 5% of the time, Pallas kernels for 0%

commit v1 on v0

--- a/solution.py
+++ b/solution.py
@@ -116,7 +116,7 @@
             preferred_element_type=jnp.float32,
         )
         adjoint = adjoint + back
-    weight_grads = lax.psum(jnp.stack(grad_list, 0), ("row", "col"))
+    weight_grads = lax.psum(lax.psum(jnp.stack(grad_list, 0), "row"), "col")
     transposed = coarse_map.T
     back_map = jnp.where(is_last, zero_map, transposed)
     back_offset = jnp.where(is_last, adjoint, adjoint - exact_dot(transposed, guess_flat))

time: 563 us -> 523 us (0.929)
  waiting for transfers between devices: 312 us -> 271 us
    psum x1 -> x2, waiting for transfers between devices: 110 us -> 78.7 us  [local(): weight_grads = lax.psum(lax.psum(jnp.stack(grad_list, 0), 'row'), 'col')]
    ppermute x14, waiting for transfers between devices: 88.8 us -> 77.6 us  [from_behind(): return lax.ppermute(array, axis, pairs)]
  transfers between devices with their start and end apart: 63 -> 64, of which waited for: 49 -> 50; matrix products, arithmetic and copies ran while one was open for 5% -> 6% of each run, Pallas kernels for 0% -> 0%
where the time goes in v1:
time: 523 us; the launch traced here: 517 us
  waiting for transfers between devices  271 us (52%)
  starting transfers between devices  164 us (31%)
  local copies, waits for them, and re-layouts  28.5 us (5%)
  other arithmetic  23.8 us (5%)
  between operations  16.2 us (3%)
  matrix products  13.6 us (3%)
    ppermute x24, waiting for transfers between devices, with_halo(): lax.ppermute(head, axis, [((i + 1) % count, i) for i in range(ends)])  79.1 us
    psum x2, waiting for transfers between devices, local(): weight_grads = lax.psum(lax.psum(jnp.stack(grad_list, 0), 'row'), 'col')  78.7 us
    ppermute x14, waiting for transfers between devices, from_behind(): return lax.ppermute(array, axis, pairs)  77.6 us
    ppermute x24, starting transfers between devices, with_halo(): lax.ppermute(tail, axis, [(i, (i + 1) % count) for i in range(ends)])  77.1 us
    ppermute x24, starting transfers between devices, with_halo(): lax.ppermute(head, axis, [((i + 1) % count, i) for i in range(ends)])  45.3 us
    ppermute x14, starting transfers between devices, from_behind(): return lax.ppermute(array, axis, pairs)  41.3 us
    ppermute x24, waiting for transfers between devices, with_halo(): lax.ppermute(tail, axis, [(i, (i + 1) % count) for i in range(ends)])  35.5 us
    concatenate x36, other arithmetic, with_halo(): jnp.concatenate([lax.ppermute(tail, axis, [(i, (i + 1) % count) for i in...  20.8 us
  transfers between devices with their start and end apart: 64, of which 50 were waited for; matrix products, arithmetic and copies ran while one was open for 6% of the time, Pallas kernels for 0%

profile of v1, /device:TPU:1, one launch (start us, length us, event | category | flops | bytes accessed | tf_op | source)
XLA Modules:
  0.0 517.0 jit_solution(17134181764418137147)
XLA Ops:
  12.8 5.6 %collective-permute-start.3 = (bf16[64,1,128]{2,1,0:T(2,128)(2,1)S(1)}, bf16[64,1,128]{2,1,0:T(2,128)(2,1)S(1)}, u32[]{:S(2)}, u32[]{:S(2)}) collective-permute-start(bf16[64,1,128]{2,1,0:T(2,128)(2,1)S(1)} %get-tuple-element.224), channel_id=1, source_target_pairs={{8,0},{16,8},{24,16},{32,24},{40,32},{48,40},{56,48},{9,1},{17,9},... | collective-permute-start | bytes 49160 | tf_op jit(solution)/shard_map/ppermute | solution.py:19
  22.8 4.6 collective-permute-done.4
  64.7 5.2 %collective-permute-start.12 = (bf16[64,10,1]{2,1,0:T(8,128)(2,1)S(1)}, bf16[64,10,1]{2,1,0:T(8,128)(2,1)S(1)}, u32[]{:S(2)}, u32[]{:S(2)}) collective-permute-start(bf16[64,10,1]{2,1,0:T(8,128)(2,1)S(1)} %get-tuple-element.172), channel_id=1, source_target_pairs={{0,1},{1,2},{2,3},{3,4},{4,5},{5,6},{6,7},{8,9},{9,10},{10,11},{11... | collective-permute-start | bytes 3848 | tf_op jit(solution)/shard_map/ppermute | solution.py:17
  74.9 4.8 collective-permute-done.13
  105.2 64.1 %while.20 = (s32[]{:T(128)}, f32[64,1024]{1,0:T(8,128)S(1)}, f32[64,64]{1,0:T(8,128)S(1)}, f32[64,1024]{1,0:T(8,128)S(1)}, s32[]{:T(128)}) while((s32[]{:T(128)}, f32[64,1024]{1,0:T(8,128)S(1)}, f32[64,64]{1,0:T(8,128)S(1)}, f32[64,1024]{1,0:T(8,128)S(1)}, s32[]{:T(128)}) %tuple.143), condition=%wide.region_2.3_spmd, body=%wide.region_1.2_spmd.sunk | while | flops 50397184 | bytes 1851493 | solution.py:91
  109.6 5.8 %collective-permute-done = f32[64,1024]{1,0:T(8,128)S(1)} collective-permute-done((f32[64,1024]{1,0:T(8,128)S(1)}, f32[64,1024]{1,0:T(8,128)S(1)}, u32[]{:S(2)}, u32[]{:S(2)}) %collective-permute-start) | collective-permute-done | bytes 262176 | tf_op jit(solution)/shard_map/while/body/eval_jaxpr/ppermute | solution.py:29
  119.8 5.4 %collective-permute-done = f32[64,1024]{1,0:T(8,128)S(1)} collective-permute-done((f32[64,1024]{1,0:T(8,128)S(1)}, f32[64,1024]{1,0:T(8,128)S(1)}, u32[]{:S(2)}, u32[]{:S(2)}) %collective-permute-start) | collective-permute-done | bytes 262176 | tf_op jit(solution)/shard_map/while/body/eval_jaxpr/ppermute | solution.py:29
  134.6 5.4 %collective-permute-start = (f32[64,1024]{1,0:T(8,128)S(1)}, f32[64,1024]{1,0:T(8,128)S(1)}, u32[]{:S(2)}, u32[]{:S(2)}) collective-permute-start(f32[64,1024]{1,0:T(8,128)S(1)} %convolution_add_fusion.4), channel_id=1, source_target_pairs={{0,64},{64,128},{128,192},{192,256},{256,320},{320,384},{384,448},... | collective-permute-start | bytes 786440 | tf_op jit(solution)/shard_map/while/body/eval_jaxpr/ppermute | solution.py:29
  151.8 5.3 %collective-permute-start = (f32[64,1024]{1,0:T(8,128)S(1)}, f32[64,1024]{1,0:T(8,128)S(1)}, u32[]{:S(2)}, u32[]{:S(2)}) collective-permute-start(f32[64,1024]{1,0:T(8,128)S(1)} %convolution_add_fusion.4), channel_id=1, source_target_pairs={{0,64},{64,128},{128,192},{192,256},{256,320},{320,384},{384,448},... | collective-permute-start | bytes 786440 | tf_op jit(solution)/shard_map/while/body/eval_jaxpr/ppermute | solution.py:29
  160.8 5.3 %collective-permute-start = (f32[64,1024]{1,0:T(8,128)S(1)}, f32[64,1024]{1,0:T(8,128)S(1)}, u32[]{:S(2)}, u32[]{:S(2)}) collective-permute-start(f32[64,1024]{1,0:T(8,128)S(1)} %convolution_add_fusion.4), channel_id=1, source_target_pairs={{0,64},{64,128},{128,192},{192,256},{256,320},{320,384},{384,448},... | collective-permute-start | bytes 786440 | tf_op jit(solution)/shard_map/while/body/eval_jaxpr/ppermute | solution.py:29
  169.5 6.1 %collective-permute-start.18 = (bf16[64,1,128]{2,1,0:T(2,128)(2,1)S(1)}, bf16[64,1,128]{2,1,0:T(2,128)(2,1)S(1)}, u32[]{:S(2)}, u32[]{:S(2)}) collective-permute-start(bf16[64,1,128]{2,1,0:T(2,128)(2,1)S(1)} %get-tuple-element.215), channel_id=1, source_target_pairs={{0,8},{8,16},{16,24},{24,32},{32,40},{40,48},{48,56},{1,9},{9,17},... | collective-permute-start | bytes 49160 | tf_op jit(solution)/shard_map/ppermute | solution.py:17
  210.9 4.8 collective-permute-done.25
  288.0 6.2 %collective-permute-done.37 = bf16[64,10,1]{2,1,0:T(8,128)(2,1)S(1)} collective-permute-done((bf16[64,10,1]{2,1,0:T(8,128)(2,1)}, bf16[64,10,1]{2,1,0:T(8,128)(2,1)S(1)}, u32[]{:S(2)}, u32[]{:S(2)}) %collective-permute-start.37) | collective-permute-done | bytes 1312 | tf_op jit(solution)/shard_map/ppermute | solution.py:19
  361.7 4.6 collective-permute-done.49
  368.6 61.6 %all-reduce.3.cloned.1.call-done = f32[4,64,576]{2,1,0:T(8,128)} async-done(((f32[4,64,576]{2,1,0:T(8,128)}), f32[4,64,576]{2,1,0:T(8,128)}) %all-reduce.3.cloned.1.call-update) | async-done | bytes 589840 | tf_op jit(solution)/shard_map/psum | solution.py:119
  430.3 60.0 %while.21 = (s32[]{:T(128)}, f32[64,1024]{1,0:T(8,128)S(1)}, f32[64,64]{1,0:T(8,128)S(1)}, f32[64,1024]{1,0:T(8,128)S(1)}, s32[]{:T(128)}) while((s32[]{:T(128)}, f32[64,1024]{1,0:T(8,128)S(1)}, f32[64,64]{1,0:T(8,128)S(1)}, f32[64,1024]{1,0:T(8,128)S(1)}, s32[]{:T(128)}) %tuple.146), condition=%wide.region_4.5_spmd, body=%wide.region_3.4_spmd.sunk | while | flops 50397184 | bytes 1851493 | solution.py:127
  432.0 6.2 %collective-permute-done.1 = f32[64,1024]{1,0:T(8,128)S(1)} collective-permute-done((f32[64,1024]{1,0:T(8,128)S(1)}, f32[64,1024]{1,0:T(8,128)S(1)}, u32[]{:S(2)}, u32[]{:S(2)}) %collective-permute-start.1) | collective-permute-done | bytes 262176 | tf_op jit(solution)/shard_map/while/body/eval_jaxpr/ppermute | solution.py:29
  439.8 5.8 %collective-permute-done.1 = f32[64,1024]{1,0:T(8,128)S(1)} collective-permute-done((f32[64,1024]{1,0:T(8,128)S(1)}, f32[64,1024]{1,0:T(8,128)S(1)}, u32[]{:S(2)}, u32[]{:S(2)}) %collective-permute-start.1) | collective-permute-done | bytes 262176 | tf_op jit(solution)/shard_map/while/body/eval_jaxpr/ppermute | solution.py:29
  447.3 6.2 %collective-permute-done.1 = f32[64,1024]{1,0:T(8,128)S(1)} collective-permute-done((f32[64,1024]{1,0:T(8,128)S(1)}, f32[64,1024]{1,0:T(8,128)S(1)}, u32[]{:S(2)}, u32[]{:S(2)}) %collective-permute-start.1) | collective-permute-done | bytes 262176 | tf_op jit(solution)/shard_map/while/body/eval_jaxpr/ppermute | solution.py:29
  455.2 6.2 %collective-permute-done.1 = f32[64,1024]{1,0:T(8,128)S(1)} collective-permute-done((f32[64,1024]{1,0:T(8,128)S(1)}, f32[64,1024]{1,0:T(8,128)S(1)}, u32[]{:S(2)}, u32[]{:S(2)}) %collective-permute-start.1) | collective-permute-done | bytes 262176 | tf_op jit(solution)/shard_map/while/body/eval_jaxpr/ppermute | solution.py:29
  463.1 6.5 %collective-permute-done.1 = f32[64,1024]{1,0:T(8,128)S(1)} collective-permute-done((f32[64,1024]{1,0:T(8,128)S(1)}, f32[64,1024]{1,0:T(8,128)S(1)}, u32[]{:S(2)}, u32[]{:S(2)}) %collective-permute-start.1) | collective-permute-done | bytes 262176 | tf_op jit(solution)/shard_map/while/body/eval_jaxpr/ppermute | solution.py:29
  471.3 7.8 %collective-permute-done.1 = f32[64,1024]{1,0:T(8,128)S(1)} collective-permute-done((f32[64,1024]{1,0:T(8,128)S(1)}, f32[64,1024]{1,0:T(8,128)S(1)}, u32[]{:S(2)}, u32[]{:S(2)}) %collective-permute-start.1) | collective-permute-done | bytes 262176 | tf_op jit(solution)/shard_map/while/body/eval_jaxpr/ppermute | solution.py:29
  480.7 9.6 %collective-permute-done.1 = f32[64,1024]{1,0:T(8,128)S(1)} collective-permute-done((f32[64,1024]{1,0:T(8,128)S(1)}, f32[64,1024]{1,0:T(8,128)S(1)}, u32[]{:S(2)}, u32[]{:S(2)}) %collective-permute-start.1) | collective-permute-done | bytes 262176 | tf_op jit(solution)/shard_map/while/body/eval_jaxpr/ppermute | solution.py:29
  491.1 17.1 %all-reduce.5.cloned.1.call-done = f32[4,64,576]{2,1,0:T(8,128)} async-done(((f32[4,64,576]{2,1,0:T(8,128)}), f32[4,64,576]{2,1,0:T(8,128)}) %all-reduce.5.cloned.1.call-update) | async-done | bytes 589840 | tf_op jit(solution)/shard_map/psum | solution.py:119
  (403 shorter events, 304.4 us)
Async XLA Ops:
  7.2 423.1 %all-reduce.3.cloned.1.call-start = ((), (), s32[]{:S(2)}) async-start(), calls=%async_computation | async-start | bytes 1310720 | tf_op jit(solution)/shard_map/psum | solution.py:119
  8.2 10.1 %collective-permute-start.2 = (bf16[64,1,128]{2,1,0:T(2,128)(2,1)S(1)}, bf16[64,1,128]{2,1,0:T(2,128)(2,1)S(1)}, u32[]{:S(2)}, u32[]{:S(2)}) collective-permute-start(bf16[64,1,128]{2,1,0:T(2,128)(2,1)S(1)} %get-tuple-element.223), channel_id=1, source_target_pairs={{0,8},{8,16},{16,24},{24,32},{32,40},{40,48},{48,56},{1,9},{9,17},... | collective-permute-start | bytes 49160 | tf_op jit(solution)/shard_map/ppermute | solution.py:17
  21.5 10.1 %collective-permute-start.5 = (bf16[64,10,1]{2,1,0:T(8,128)(2,1)S(1)}, bf16[64,10,1]{2,1,0:T(8,128)(2,1)S(1)}, u32[]{:S(2)}, u32[]{:S(2)}) collective-permute-start(bf16[64,10,1]{2,1,0:T(8,128)(2,1)S(1)} %get-tuple-element.175), channel_id=1, source_target_pairs={{1,0},{2,1},{3,2},{4,3},{5,4},{6,5},{7,6},{9,8},{10,9},{11,10},{12... | collective-permute-start | bytes 3848 | tf_op jit(solution)/shard_map/ppermute | solution.py:19
  64.7 9.7 %collective-permute-start.12 = (bf16[64,10,1]{2,1,0:T(8,128)(2,1)S(1)}, bf16[64,10,1]{2,1,0:T(8,128)(2,1)S(1)}, u32[]{:S(2)}, u32[]{:S(2)}) collective-permute-start(bf16[64,10,1]{2,1,0:T(8,128)(2,1)S(1)} %get-tuple-element.172), channel_id=1, source_target_pairs={{0,1},{1,2},{2,3},{3,4},{4,5},{5,6},{6,7},{8,9},{9,10},{10,11},{11... | collective-permute-start | bytes 3848 | tf_op jit(solution)/shard_map/ppermute | solution.py:17
  70.8 8.9 %collective-permute-start.13 = (bf16[64,10,1]{2,1,0:T(8,128)(2,1)S(1)}, bf16[64,10,1]{2,1,0:T(8,128)(2,1)S(1)}, u32[]{:S(2)}, u32[]{:S(2)}) collective-permute-start(bf16[64,10,1]{2,1,0:T(8,128)(2,1)S(1)} %get-tuple-element.171), channel_id=1, source_target_pairs={{1,0},{2,1},{3,2},{4,3},{5,4},{6,5},{7,6},{9,8},{10,9},{11,10},{12... | collective-permute-start | bytes 3848 | tf_op jit(solution)/shard_map/ppermute | solution.py:19
  105.6 9.8 %collective-permute-start = (f32[64,1024]{1,0:T(8,128)S(1)}, f32[64,1024]{1,0:T(8,128)S(1)}, u32[]{:S(2)}, u32[]{:S(2)}) collective-permute-start(f32[64,1024]{1,0:T(8,128)S(1)} %convolution_add_fusion.4), channel_id=1, source_target_pairs={{0,64},{64,128},{128,192},{192,256},{256,320},{320,384},{384,448},... | collective-permute-start | bytes 786440 | tf_op jit(solution)/shard_map/while/body/eval_jaxpr/ppermute | solution.py:29
  115.8 9.4 %collective-permute-start = (f32[64,1024]{1,0:T(8,128)S(1)}, f32[64,1024]{1,0:T(8,128)S(1)}, u32[]{:S(2)}, u32[]{:S(2)}) collective-permute-start(f32[64,1024]{1,0:T(8,128)S(1)} %convolution_add_fusion.4), channel_id=1, source_target_pairs={{0,64},{64,128},{128,192},{192,256},{256,320},{320,384},{384,448},... | collective-permute-start | bytes 786440 | tf_op jit(solution)/shard_map/while/body/eval_jaxpr/ppermute | solution.py:29
  125.6 8.6 %collective-permute-start = (f32[64,1024]{1,0:T(8,128)S(1)}, f32[64,1024]{1,0:T(8,128)S(1)}, u32[]{:S(2)}, u32[]{:S(2)}) collective-permute-start(f32[64,1024]{1,0:T(8,128)S(1)} %convolution_add_fusion.4), channel_id=1, source_target_pairs={{0,64},{64,128},{128,192},{192,256},{256,320},{320,384},{384,448},... | collective-permute-start | bytes 786440 | tf_op jit(solution)/shard_map/while/body/eval_jaxpr/ppermute | solution.py:29
  134.6 9.1 %collective-permute-start = (f32[64,1024]{1,0:T(8,128)S(1)}, f32[64,1024]{1,0:T(8,128)S(1)}, u32[]{:S(2)}, u32[]{:S(2)}) collective-permute-start(f32[64,1024]{1,0:T(8,128)S(1)} %convolution_add_fusion.4), channel_id=1, source_target_pairs={{0,64},{64,128},{128,192},{192,256},{256,320},{320,384},{384,448},... | collective-permute-start | bytes 786440 | tf_op jit(solution)/shard_map/while/body/eval_jaxpr/ppermute | solution.py:29
  160.8 8.6 %collective-permute-start = (f32[64,1024]{1,0:T(8,128)S(1)}, f32[64,1024]{1,0:T(8,128)S(1)}, u32[]{:S(2)}, u32[]{:S(2)}) collective-permute-start(f32[64,1024]{1,0:T(8,128)S(1)} %convolution_add_fusion.4), channel_id=1, source_target_pairs={{0,64},{64,128},{128,192},{192,256},{256,320},{320,384},{384,448},... | collective-permute-start | bytes 786440 | tf_op jit(solution)/shard_map/while/body/eval_jaxpr/ppermute | solution.py:29
  169.5 9.0 %collective-permute-start.18 = (bf16[64,1,128]{2,1,0:T(2,128)(2,1)S(1)}, bf16[64,1,128]{2,1,0:T(2,128)(2,1)S(1)}, u32[]{:S(2)}, u32[]{:S(2)}) collective-permute-start(bf16[64,1,128]{2,1,0:T(2,128)(2,1)S(1)} %get-tuple-element.215), channel_id=1, source_target_pairs={{0,8},{8,16},{16,24},{24,32},{32,40},{40,48},{48,56},{1,9},{9,17},... | collective-permute-start | bytes 49160 | tf_op jit(solution)/shard_map/ppermute | solution.py:17
  183.3 9.5 %collective-permute-start.21 = (bf16[64,10,1]{2,1,0:T(8,128)(2,1)S(1)}, bf16[64,10,1]{2,1,0:T(8,128)(2,1)S(1)}, u32[]{:S(2)}, u32[]{:S(2)}) collective-permute-start(bf16[64,10,1]{2,1,0:T(8,128)(2,1)S(1)} %get-tuple-element.167), channel_id=1, source_target_pairs={{1,0},{2,1},{3,2},{4,3},{5,4},{6,5},{7,6},{9,8},{10,9},{11,10},{12... | collective-permute-start | bytes 3848 | tf_op jit(solution)/shard_map/ppermute | solution.py:19
  206.0 9.8 %collective-permute-start.25 = (bf16[64,10,1]{2,1,0:T(8,128)(2,1)S(1)}, bf16[64,10,1]{2,1,0:T(8,128)(2,1)S(1)}, u32[]{:S(2)}, u32[]{:S(2)}) collective-permute-start(bf16[64,10,1]{2,1,0:T(8,128)(2,1)S(1)} %get-tuple-element.165), channel_id=1, source_target_pairs={{1,0},{2,1},{3,2},{4,3},{5,4},{6,5},{7,6},{9,8},{10,9},{11,10},{12... | collective-permute-start | bytes 3848 | tf_op jit(solution)/shard_map/ppermute | solution.py:19
  231.3 8.8 %collective-permute-start.29 = (bf16[64,10,1]{2,1,0:T(8,128)(2,1)}, bf16[64,10,1]{2,1,0:T(8,128)(2,1)S(1)}, u32[]{:S(2)}, u32[]{:S(2)}) collective-permute-start(bf16[64,10,1]{2,1,0:T(8,128)(2,1)} %get-tuple-element.163), channel_id=1, source_target_pairs={{1,0},{2,1},{3,2},{4,3},{5,4},{6,5},{7,6},{9,8},{10,9},{11,10},{12... | collective-permute-start | bytes 3848 | tf_op jit(solution)/shard_map/ppermute | solution.py:19
  255.5 8.7 %collective-permute-start.33 = (bf16[64,10,1]{2,1,0:T(8,128)(2,1)}, bf16[64,10,1]{2,1,0:T(8,128)(2,1)S(1)}, u32[]{:S(2)}, u32[]{:S(2)}) collective-permute-start(bf16[64,10,1]{2,1,0:T(8,128)(2,1)} %get-tuple-element.161), channel_id=1, source_target_pairs={{1,0},{2,1},{3,2},{4,3},{5,4},{6,5},{7,6},{9,8},{10,9},{11,10},{12... | collective-permute-start | bytes 3848 | tf_op jit(solution)/shard_map/ppermute | solution.py:19
  277.5 8.7 %collective-permute-start.36 = (bf16[64,10,1]{2,1,0:T(8,128)(2,1)}, bf16[64,10,1]{2,1,0:T(8,128)(2,1)}, u32[]{:S(2)}, u32[]{:S(2)}) collective-permute-start(bf16[64,10,1]{2,1,0:T(8,128)(2,1)} %get-tuple-element.160), channel_id=1, source_target_pairs={{0,1},{1,2},{2,3},{3,4},{4,5},{5,6},{6,7},{8,9},{9,10},{10,11},{11... | collective-permute-start | bytes 3848 | tf_op jit(solution)/shard_map/ppermute | solution.py:17
  285.0 9.3 %collective-permute-start.37 = (bf16[64,10,1]{2,1,0:T(8,128)(2,1)}, bf16[64,10,1]{2,1,0:T(8,128)(2,1)S(1)}, u32[]{:S(2)}, u32[]{:S(2)}) collective-permute-start(bf16[64,10,1]{2,1,0:T(8,128)(2,1)} %get-tuple-element.159), channel_id=1, source_target_pairs={{1,0},{2,1},{3,2},{4,3},{5,4},{6,5},{7,6},{9,8},{10,9},{11,10},{12... | collective-permute-start | bytes 3848 | tf_op jit(solution)/shard_map/ppermute | solution.py:19
  298.6 9.9 %collective-permute-start.38 = (bf16[64,1,128]{2,1,0:T(2,128)(2,1)}, bf16[64,1,128]{2,1,0:T(2,128)(2,1)S(1)}, u32[]{:S(2)}, u32[]{:S(2)}) collective-permute-start(bf16[64,1,128]{2,1,0:T(2,128)(2,1)} %get-tuple-element.205), channel_id=1, source_target_pairs={{0,8},{8,16},{16,24},{24,32},{32,40},{40,48},{48,56},{1,9},{9,17},... | collective-permute-start | bytes 49160 | tf_op jit(solution)/shard_map/ppermute | solution.py:17
  311.8 9.9 %collective-permute-start.41 = (bf16[64,10,1]{2,1,0:T(8,128)(2,1)S(1)}, bf16[64,10,1]{2,1,0:T(8,128)(2,1)S(1)}, u32[]{:S(2)}, u32[]{:S(2)}) collective-permute-start(bf16[64,10,1]{2,1,0:T(8,128)(2,1)S(1)} %get-tuple-element.157), channel_id=1, source_target_pairs={{1,0},{2,1},{3,2},{4,3},{5,4},{6,5},{7,6},{9,8},{10,9},{11,10},{12... | collective-permute-start | bytes 3848 | tf_op jit(solution)/shard_map/ppermute | solution.py:19
  334.8 9.0 %collective-permute-start.45 = (bf16[64,10,1]{2,1,0:T(8,128)(2,1)S(1)}, bf16[64,10,1]{2,1,0:T(8,128)(2,1)S(1)}, u32[]{:S(2)}, u32[]{:S(2)}) collective-permute-start(bf16[64,10,1]{2,1,0:T(8,128)(2,1)S(1)} %get-tuple-element.155), channel_id=1, source_target_pairs={{1,0},{2,1},{3,2},{4,3},{5,4},{6,5},{7,6},{9,8},{10,9},{11,10},{12... | collective-permute-start | bytes 3848 | tf_op jit(solution)/shard_map/ppermute | solution.py:19
  357.1 151.0 %all-reduce.5.cloned.1.call-start = ((), (), s32[]{:S(2)}) async-start(), calls=%async_computation.1 | async-start | bytes 1310720 | tf_op jit(solution)/shard_map/psum | solution.py:119
  357.2 9.0 %collective-permute-start.49 = (bf16[64,10,1]{2,1,0:T(8,128)(2,1)S(1)}, bf16[64,10,1]{2,1,0:T(8,128)(2,1)S(1)}, u32[]{:S(2)}, u32[]{:S(2)}) collective-permute-start(bf16[64,10,1]{2,1,0:T(8,128)(2,1)S(1)} %get-tuple-element.153), channel_id=1, source_target_pairs={{1,0},{2,1},{3,2},{4,3},{5,4},{6,5},{7,6},{9,8},{10,9},{11,10},{12... | collective-permute-start | bytes 3848 | tf_op jit(solution)/shard_map/ppermute | solution.py:19
  470.0 9.1 %collective-permute-start.1 = (f32[64,1024]{1,0:T(8,128)S(1)}, f32[64,1024]{1,0:T(8,128)S(1)}, u32[]{:S(2)}, u32[]{:S(2)}) collective-permute-start(f32[64,1024]{1,0:T(8,128)S(1)} %convolution_add_fusion.5), channel_id=1, source_target_pairs={{64,0},{128,64},{192,128},{256,192},{320,256},{384,320},{448,384},... | collective-permute-start | bytes 786440 | tf_op jit(solution)/shard_map/while/body/eval_jaxpr/ppermute | solution.py:29
  479.4 10.9 %collective-permute-start.1 = (f32[64,1024]{1,0:T(8,128)S(1)}, f32[64,1024]{1,0:T(8,128)S(1)}, u32[]{:S(2)}, u32[]{:S(2)}) collective-permute-start(f32[64,1024]{1,0:T(8,128)S(1)} %convolution_add_fusion.5), channel_id=1, source_target_pairs={{64,0},{128,64},{192,128},{256,192},{320,256},{384,320},{448,384},... | collective-permute-start | bytes 786440 | tf_op jit(solution)/shard_map/while/body/eval_jaxpr/ppermute | solution.py:29
  (67 other events, 427.0 us)
Sparse Core Ops, SparseCore 0:
  357.3 72.9 all-reduce.2
  432.6 75.5 all-reduce.4
